TPU v7x, 32 devices: a whole 2x2x4 slice. The times are simulated.
32 devices in a mesh: grid: 8 (over z, x), cols: 4 (over y, core).
Axes of the slice: x: 2, y: 2, z: 4, core: 2. Of those that a mesh axis runs over, the one named last changes fastest.
Arguments:
- basis: float32 [1024, 3, 16, 1024], P('cols', None, 'grid'), may hold values from -1 to 1
- snapshots: float32 [128, 3, 16, 1024], P('cols', None, 'grid'), may hold values from -60 to 60
- permittivity: float32 [3, 16, 1024], P(None, 'grid'), may hold values from 1 to 10
- labels: int32 [16, 1024], P('grid'), may hold values from 0 to 7
- sigma_table: float32 [8], replicated, may hold values from 0.1 to 10
Outputs:
- new_basis: float32 [128, 3, 16, 1024], P('cols', None, 'grid')
- coefficients: float32 [1024, 128], P('cols')
- cross_terms: float32 [3, 1024, 128], P(None, 'cols')
- block_terms: float32 [3, 128, 128], P(None, 'cols')
All inputs are finite; a program needn't handle non-finite values.
Results may differ from a plain program's by a relative error of at most 0.0003.
Values sent between devices are 32-bit elements; how exact they have to be, the bound alone decides.
A program may use at most 128 MiB of HBM per device.

v0:
```python
import jax
import jax.numpy as jnp
from jax import lax
from jax.sharding import PartitionSpec as P

NY = 32
HIGHEST = lax.Precision.HIGHEST


def padded(shard, sides, width):
    for axis, dim in sides:
        size, length = (lax.axis_size(axis), shard.shape[dim])
        up = [(i, (i + 1) % size) for i in range(size - 1)]
        down = [(j, i) for i, j in up]
        last = lax.slice_in_dim(shard, length - width, length, axis=dim)
        leading = lax.slice_in_dim(shard, 0, width, axis=dim)
        before = lax.ppermute(last, axis, up)
        after = lax.ppermute(leading, axis, down)
        shard = jnp.concatenate([before, shard, after], axis=dim)
    return shard


def cells_dot(left_rows, right_rows):
    left_flat = left_rows.reshape(left_rows.shape[0], -1)
    right_flat = right_rows.reshape(right_rows.shape[0], -1)
    return lax.dot_general(
        left_flat,
        right_flat,
        (((1,), (1,)), ((), ())),
        precision=HIGHEST,
        preferred_element_type=jnp.float32,
    )


def combine_rows(weights, fields):
    flattened = fields.reshape(fields.shape[0], -1)
    output_rows = lax.dot_general(
        weights,
        flattened,
        (((0,), (0,)), ((), ())),
        precision=HIGHEST,
        preferred_element_type=jnp.float32,
    )
    return output_rows.reshape((weights.shape[1],) + fields.shape[1:])


def forward_x(field, row_len):
    padding_cols = jnp.zeros(field.shape[:-1] + (row_len,), field.dtype)
    return jnp.concatenate([field[..., row_len:], padding_cols], axis=-1)


def backward_x(field, row_len):
    padding_cols = jnp.zeros(field.shape[:-1] + (row_len,), field.dtype)
    return jnp.concatenate([padding_cols, field[..., :-row_len]], axis=-1)


def forward_y(field, row_len):
    column_pos = lax.broadcasted_iota(jnp.int32, (field.shape[-1],), 0) % row_len
    padding_cols = jnp.zeros(field.shape[:-1] + (1,), field.dtype)
    shifted = jnp.concatenate([field[..., 1:], padding_cols], axis=-1)
    return jnp.where(column_pos != row_len - 1, shifted, 0.0)


def backward_y(field, row_len):
    column_pos = lax.broadcasted_iota(jnp.int32, (field.shape[-1],), 0) % row_len
    padding_cols = jnp.zeros(field.shape[:-1] + (1,), field.dtype)
    shifted = jnp.concatenate([padding_cols, field[..., :-1]], axis=-1)
    return jnp.where(column_pos != 0, shifted, 0.0)


def curl_curl(extended, row_len):
    field_x = extended[:, 0]
    field_y = extended[:, 1]
    field_z = extended[:, 2]

    def middle(field):
        return field[:, 1:-1]

    def plus_x(field):
        return forward_x(field, row_len) - field

    def minus_x(field):
        return field - backward_x(field, row_len)

    def plus_y(field):
        return forward_y(field, row_len) - field

    def minus_y(field):
        return field - backward_y(field, row_len)

    def second_x(field):
        return forward_x(field, row_len) - 2.0 * field + backward_x(field, row_len)

    def second_y(field):
        return forward_y(field, row_len) - 2.0 * field + backward_y(field, row_len)

    def second_z(field):
        return field[:, 2:] - 2.0 * field[:, 1:-1] + field[:, :-2]

    curl_x = (
        -second_y(middle(field_x))
        - second_z(field_x)
        + minus_y(plus_x(middle(field_y)))
        + plus_x(middle(field_z))
        - plus_x(field_z[:, :-2])
    )
    curl_y = (
        -second_x(middle(field_y))
        - second_z(field_y)
        + minus_x(plus_y(middle(field_x)))
        + plus_y(middle(field_z))
        - plus_y(field_z[:, :-2])
    )
    curl_z = (
        -second_x(middle(field_z))
        - second_y(middle(field_z))
        + minus_x(field_x[:, 2:] - middle(field_x))
        + minus_y(field_y[:, 2:] - middle(field_y))
    )
    return jnp.stack([curl_x, curl_y, curl_z], axis=1)


def lookup_sigma(labels, sigma_table):
    region_ids = jnp.arange(sigma_table.shape[0], dtype=jnp.int32)
    picked = jnp.where(labels[None] == region_ids[:, None, None], sigma_table[:, None, None], 0.0)
    return jnp.sum(picked, axis=0)


def apply_ops(fields, permittivity, conductivity):
    extended = padded(fields, (("grid", 2),), 1)
    curl_term = curl_curl(extended, NY)
    mass_term = permittivity[None] * fields
    loss_term = conductivity[None, None] * fields
    return (curl_term, mass_term, loss_term)


def shards(basis, snapshots, permittivity, labels, sigma_table):
    basis_cols = basis.shape[0]
    snap_cols = snapshots.shape[0]
    total_snap = snap_cols * lax.axis_size("cols")
    unknowns = 3 * snapshots.shape[3] * snapshots.shape[2] * lax.axis_size("grid")
    conductivity = lookup_sigma(labels, sigma_table)
    current = snapshots
    coefficients = jnp.zeros((basis_cols, total_snap), jnp.float32)
    for sweep_index in range(2):
        partial_value = cells_dot(basis, lax.all_gather(current, "cols", axis=0, tiled=True))
        coef_part = lax.psum(partial_value, "grid")
        current = current - lax.psum_scatter(
            combine_rows(coef_part, basis), "cols", scatter_dimension=0, tiled=True
        )
        coefficients = coefficients + coef_part
    finished = lax.all_gather(current, "cols", axis=0, tiled=True)
    own_start = lax.axis_index("cols") * snap_cols
    identity = jnp.eye(total_snap, dtype=jnp.float32)
    gram_sum = lax.psum(cells_dot(finished, finished) / unknowns, "grid")
    lower_factor = jnp.linalg.cholesky(gram_sum)
    inverse = jax.scipy.linalg.solve_triangular(lower_factor, identity, lower=True)
    new_all = combine_rows(inverse.T, finished)
    curl_term, mass_term, loss_term = apply_ops(new_all, permittivity, conductivity)
    own_new = lax.dynamic_slice_in_dim(new_all, own_start, snap_cols, 0)
    cross_part = jnp.stack(
        [cells_dot(basis, curl_term), cells_dot(basis, mass_term), cells_dot(basis, loss_term)],
        axis=0,
    )
    block_part = (
        jnp.stack(
            [
                cells_dot(own_new, curl_term),
                cells_dot(own_new, mass_term),
                cells_dot(own_new, loss_term),
            ],
            axis=0,
        )
        / unknowns
    )
    cross_terms, block_terms = lax.psum((cross_part, block_part), "grid")
    return (own_new, coefficients, cross_terms, block_terms)


def solution(mesh):
    placed = (
        P("cols", None, "grid", None),
        P("cols", None, "grid", None),
        P(None, "grid", None),
        P("grid", None),
        P(),
    )
    return jax.shard_map(
        shards,
        mesh=mesh,
        in_specs=placed,
        out_specs=(
            P("cols", None, "grid", None),
            P("cols", None),
            P(None, "cols", None),
            P(None, "cols", None),
        ),
        check_vma=False,
    )
```

profile of v0, /device:TPU:0, one launch (start us, length us, event | category | flops | bytes accessed | tf_op | source)
XLA Modules:
  0.0 642.6 jit_solution(8649278137576237144)
XLA Ops:
  7.2 2.3 copy.44
  9.5 0.0 all-reduce.19.cloned.1.call-start
  9.5 31.9 %all-gather.4.cloned.1.call-done = f32[128,3,2,1024]{3,0,2,1:T(8,128)} async-done(((f32[32,3,2,1024]{3,0,2,1:T(8,128)}), f32[128,3,2,1024]{3,0,2,1:T(8,128)}) %all-gather.4.cloned.1.call-update) | async-done | bytes 3145744 | tf_op jit(solution)/shard_map/all_gather | solution.py:146
  41.4 10.8 %fusion.23 = f32[256,128]{1,0:T(8,128)} fusion(f32[128,3,2,1024]{3,0,2,1:T(8,128)} %all-gather.4.cloned.1.call-done, f32[256,3,2,1024]{3,2,1,0:T(2,128)} %param.5), kind=kOutput, calls=%fused_computation.28 | convolution fusion | flops 2415919104 | bytes 9568256 | tf_op jit(solution)/shard_map/dot_general | solution.py:26
  52.2 0.0 reduce-scatter.3.cloned.1.call-start
  52.2 9.0 %reshape.49 = f32[256,6144]{1,0:T(8,128)} reshape(f32[256,3,2,1024]{3,2,1,0:T(2,128)} %param.5) | data formatting | bytes 12582912 | tf_op jit(solution)/shard_map/reshape | solution.py:24
  61.2 6.6 %copy.42 = f32[6144,256]{1,0:T(8,128)} copy(f32[6144,256]{0,1:T(8,128)} %bitcast.112) | data formatting | bytes 12582912 | tf_op jit(solution)/shard_map/dot_general | solution.py:37
  67.8 54.2 %all-reduce.19.cloned.1.call-done = f32[256,128]{1,0:T(8,128)} async-done(((f32[256,128]{1,0:T(8,128)}), f32[256,128]{1,0:T(8,128)}) %all-reduce.19.cloned.1.call-update) | async-done | bytes 131088 | tf_op jit(solution)/shard_map/psum | solution.py:147
  122.0 11.2 %fusion.63 = f32[128,3,2,1024]{3,0,2,1:T(8,128)} fusion(f32[3,2,1024,256]{3,2,1,0:T(8,128)} %bitcast.110, f32[256,128]{1,0:T(8,128)} %all-reduce.19.cloned.1.call-done), kind=kOutput, calls=%fused_computation.61 | convolution fusion | flops 2415919104 | bytes 9568256 | tf_op jit(solution)/shard_map/dot_general | solution.py:37
  133.3 0.3 all-gather.6.cloned.1.call-start
  133.6 37.1 %reduce-scatter.3.cloned.1.call-done = f32[32,3,2,1024]{3,0,2,1:T(8,128)} async-done(((f32[128,3,2,1024]{3,0,2,1:T(8,128)}), f32[32,3,2,1024]{3,0,2,1:T(8,128)}) %reduce-scatter.3.cloned.1.call-update) | async-done | bytes 786448 | tf_op jit(solution)/shard_map/reduce_scatter | solution.py:148
  170.7 2.3 copy_subtract_fusion
  173.0 0.0 all-reduce.21.cloned.1.call-start
  173.1 28.6 %all-gather.6.cloned.1.call-done = f32[128,3,2,1024]{3,0,2,1:T(8,128)} async-done(((f32[32,3,2,1024]{3,0,2,1:T(8,128)}), f32[128,3,2,1024]{3,0,2,1:T(8,128)}) %all-gather.6.cloned.1.call-update) | async-done | bytes 3145744 | tf_op jit(solution)/shard_map/all_gather | solution.py:146
  201.7 10.7 %fusion.26 = f32[256,128]{1,0:T(8,128)} fusion(f32[128,3,2,1024]{3,0,2,1:T(8,128)} %all-gather.6.cloned.1.call-done, f32[256,3,2,1024]{3,2,1,0:T(2,128)} %param.5), kind=kOutput, calls=%fused_computation.29 | convolution fusion | flops 2415919104 | bytes 9568256 | tf_op jit(solution)/shard_map/dot_general | solution.py:26
  212.4 0.0 reduce-scatter.5.cloned.1.call-start
  212.4 69.8 %all-reduce.21.cloned.1.call-done = f32[256,128]{1,0:T(8,128)} async-done(((f32[256,128]{1,0:T(8,128)}), f32[256,128]{1,0:T(8,128)}) %all-reduce.21.cloned.1.call-update) | async-done | bytes 131088 | tf_op jit(solution)/shard_map/psum | solution.py:147
  282.2 11.2 %fusion.61 = f32[128,3,2,1024]{3,0,2,1:T(8,128)} fusion(f32[3,2,1024,256]{3,2,1,0:T(8,128)} %bitcast.111, f32[256,128]{1,0:T(8,128)} %all-reduce.21.cloned.1.call-done), kind=kOutput, calls=%fused_computation.59 | convolution fusion | flops 2415919104 | bytes 9568256 | tf_op jit(solution)/shard_map/dot_general | solution.py:37
  293.5 0.0 all-gather.8.cloned.1.call-start
  293.5 37.3 %reduce-scatter.5.cloned.1.call-done = f32[32,3,2,1024]{3,0,2,1:T(8,128)} async-done(((f32[128,3,2,1024]{3,0,2,1:T(8,128)}), f32[32,3,2,1024]{3,0,2,1:T(8,128)}) %reduce-scatter.5.cloned.1.call-update) | async-done | bytes 786448 | tf_op jit(solution)/shard_map/reduce_scatter | solution.py:148
  330.9 2.1 sub.76
  333.0 0.4 all-reduce.23.cloned.1.call-start
  333.4 28.2 %all-gather.8.cloned.1.call-done = f32[128,3,2,1024]{3,0,2,1:T(8,128)} async-done(((f32[32,3,2,1024]{3,0,2,1:T(8,128)}), f32[128,3,2,1024]{3,0,2,1:T(8,128)}) %all-gather.8.cloned.1.call-update) | async-done | bytes 3145744 | tf_op jit(solution)/shard_map/all_gather | solution.py:152
  361.7 6.3 fusion.42
  368.0 0.0 all-reduce.25.cloned.1.call-start
  368.0 2.3 copy.50
  370.4 66.2 %all-reduce.23.cloned.1.call-done = f32[128,128]{0,1:T(8,128)} async-done(((f32[128,128]{0,1:T(8,128)}), f32[128,128]{0,1:T(8,128)}) %all-reduce.23.cloned.1.call-update) | async-done | bytes 65552 | tf_op jit(solution)/shard_map/psum | solution.py:155
  436.6 0.9 copy.49
  437.5 0.9 fusion.67
  438.4 11.7 %cholesky.17 = f32[128,128]{1,0:T(8,128)S(1)} custom-call(f32[128,128]{1,0:T(8,128)S(1)} %fusion.67), custom_call_target="Cholesky" | custom-call | tf_op jit(solution)/shard_map/jit(cholesky)/cholesky | solution.py:156
  450.1 0.6 compare_reduce_fusion
  450.8 0.7 fusion.65
  451.4 9.8 %custom-call.7 = f32[1,128,128]{1,2,0:T(8,128)S(1)} custom-call(f32[1,128,128]{2,1,0:T(8,128)S(1)} %fusion.65), custom_call_target="InvertDiagBlocksLowerTriangular" | custom-call | tf_op jit(solution)/shard_map/jit(_solve_triangular)/triangular_solve | solution.py:157
  461.3 0.2 convolution_bitcast_fusion
  461.5 4.7 fusion.10
  466.2 1.9 fusion.75
  468.1 4.5 collective-permute-start
  472.6 1.5 collective-permute-start.1
  474.1 0.1 select_reduce_fusion
  474.2 0.7 add.132
  474.9 0.1 constant_dynamic-slice_fusion
  475.0 0.9 copy-done.1
  475.8 3.1 fusion.44
  479.0 9.9 %fusion.37 = f32[1,256,128]{1,2,0:T(8,128)S(1)} fusion(f32[256,3,2,1024]{3,2,1,0:T(2,128)} %param.5, f32[128,3,2,1024]{3,0,2,1:T(8,128)S(1)} %fusion.10, f32[2,1024]{1,0:T(2,128)S(1)} %select_reduce_fusion), kind=kOutput, calls=%fused_computation.32 | convolution fusion | flops 2416705536 | bytes 9576448 | tf_op jit(solution)/shard_map/dot_general | solution.py:26
  488.9 7.2 %fusion.32 = f32[1,256,128]{1,2,0:T(8,128)S(1)} fusion(f32[256,3,2,1024]{3,2,1,0:T(2,128)S(1)} %bitcast.109, f32[128,3,2,1024]{3,0,2,1:T(8,128)S(1)} %fusion.10, f32[3,2,1024]{2,1,0:T(2,128)S(1)} %copy-done.15), kind=kOutput, calls=%fused_computation.31 | convolution fusion | flops 2416705536 | bytes 9592832 | tf_op jit(solution)/shard_map/dot_general | solution.py:26
  496.2 41.0 %collective-permute-done = f32[128,3,1,1024]{3,0,2,1:T(8,128)} collective-permute-done((f32[128,3,1,1024]{3,0,2,1:T(8,128)}, f32[128,3,1,1024]{3,0,2,1:T(8,128)}, u32[]{:S(2)}, u32[]{:S(2)}) %collective-permute-start) | collective-permute-done | bytes 1572896 | tf_op jit(solution)/shard_map/ppermute | solution.py:17
  537.2 2.7 pad_maximum_fusion
  539.9 1.1 slice_bitcast_fusion
  541.1 2.6 fusion.76
  543.7 2.4 fusion.77
  546.1 0.4 pad_subtract_fusion
  546.5 3.4 fusion.59
  549.9 1.4 fusion.54
  551.3 0.2 copy-done.8
  551.4 0.3 copy-done.11
  551.8 1.2 add_bitcast_fusion
  553.0 7.3 %fusion.29 = f32[1,256,128]{1,2,0:T(8,128)S(1)} fusion(f32[256,3,2,1024]{3,2,1,0:T(2,128)S(1)} %bitcast.109, f32[128,1,2,1024]{3,0,2,1:T(8,128)S(1)} %add_bitcast_fusion, f32[128,1,2,1024]{3,0,2,1:T(8,128)S(1)} %fusion.54, f32[128,1,2,1024]{3,0,2,1:T(8,128)S(1)} %get-tuple-element.19), kind=kOutput, calls=%fused_computation.30 | convolution fusion | flops 2417491968 | bytes 9568256 | tf_op jit(solution)/shard_map/dot_general | solution.py:26
  560.3 0.8 pad_maximum_fusion.8
  561.2 4.4 fusion.47
  565.6 1.5 copy.54
  567.1 3.1 fusion.43
  570.3 37.2 %psum.39 = f32[3,32,128]{2,1,0:T(8,128)} all-reduce(f32[3,32,128]{2,1,0:T(8,128)S(1)} %maximum_multiply_fusion), channel_id=1, replica_groups=mesh['grid'=8,'cols'=4] {'grid'}, use_global_device_ids=true, to_apply=%region_9.10 | all-reduce | flops 12288 | bytes 98304 | tf_op jit(solution)/shard_map/psum | solution.py:176
  607.5 26.2 %all-reduce.25.cloned.1.call-done = f32[3,256,128]{1,2,0:T(8,128)} async-done(((f32[3,256,128]{1,2,0:T(8,128)}), f32[3,256,128]{1,2,0:T(8,128)}) %all-reduce.25.cloned.1.call-update) | async-done | bytes 393232 | tf_op jit(solution)/shard_map/psum | solution.py:176
  633.7 1.9 copy.55
  (52 shorter events, 0.3 us)
Async XLA Ops:
  7.2 34.2 %all-gather.4.cloned.1.call-start = ((), (), s32[]{:S(2)}) async-start(), calls=%async_computation.2 | async-start | bytes 3932160 | tf_op jit(solution)/shard_map/all_gather | solution.py:146
  9.5 112.6 %all-reduce.19.cloned.1.call-start = ((), (), s32[]{:S(2)}) async-start(), calls=%async_computation.3 | async-start | bytes 262144 | tf_op jit(solution)/shard_map/psum | solution.py:147
  52.2 118.5 %reduce-scatter.3.cloned.1.call-start = ((), (), s32[]{:S(2)}) async-start(), calls=%async_computation.4 | async-start | bytes 3932160 | tf_op jit(solution)/shard_map/reduce_scatter | solution.py:148
  133.3 37.4 %copy-start.12 = (f32[32,3,2,1024]{3,2,1,0:T(2,128)S(1)}, f32[32,3,2,1024]{3,2,1,0:T(2,128)}, u32[]{:S(2)}) copy-start(f32[32,3,2,1024]{3,2,1,0:T(2,128)} %param.6) | copy-start | bytes 2359300
  133.3 68.4 %all-gather.6.cloned.1.call-start = ((), (), s32[]{:S(2)}) async-start(), calls=%async_computation.5 | async-start | bytes 3932160 | tf_op jit(solution)/shard_map/all_gather | solution.py:146
  173.0 109.2 %all-reduce.21.cloned.1.call-start = ((), (), s32[]{:S(2)}) async-start(), calls=%async_computation.6 | async-start | bytes 262144 | tf_op jit(solution)/shard_map/psum | solution.py:147
  212.4 118.5 %reduce-scatter.5.cloned.1.call-start = ((), (), s32[]{:S(2)}) async-start(), calls=%async_computation.7 | async-start | bytes 3932160 | tf_op jit(solution)/shard_map/reduce_scatter | solution.py:148
  293.5 37.4 %copy-start.3 = (f32[32,3,2,1024]{3,0,2,1:T(8,128)S(1)}, f32[32,3,2,1024]{3,0,2,1:T(8,128)}, u32[]{:S(2)}) copy-start(f32[32,3,2,1024]{3,0,2,1:T(8,128)} %copy_subtract_fusion) | copy-start | bytes 2359300
  293.5 68.2 %all-gather.8.cloned.1.call-start = ((), (), s32[]{:S(2)}) async-start(), calls=%async_computation.8 | async-start | bytes 3932160 | tf_op jit(solution)/shard_map/all_gather | solution.py:152
  333.0 103.6 %all-reduce.23.cloned.1.call-start = ((), (), s32[]{:S(2)}) async-start(), calls=%async_computation.9 | async-start | bytes 131072 | tf_op jit(solution)/shard_map/psum | solution.py:155
  361.7 6.4 copy-start
  368.0 265.7 %all-reduce.25.cloned.1.call-start = ((), (), s32[]{:S(2)}) async-start(), calls=%async_computation.10 | async-start | bytes 786432 | tf_op jit(solution)/shard_map/psum | solution.py:176
  466.2 7.9 %copy-start.16 = (s32[2,1024]{1,0:T(2,128)S(1)}, s32[2,1024]{1,0:T(2,128)}, u32[]{:S(2)}) copy-start(s32[2,1024]{1,0:T(2,128)} %param.8) | copy-start | bytes 24580
  466.2 7.9 %copy-start.17 = (f32[8]{0:T(128)S(1)}, f32[8]{0:T(128)}, u32[]{:S(2)}) copy-start(f32[8]{0:T(128)} %param.9) | copy-start | bytes 100
  466.2 8.0 %copy-start.13 = (f32[256,128]{1,0:T(8,128)S(1)}, f32[256,128]{1,0:T(8,128)}, u32[]{:S(2)}) copy-start(f32[256,128]{1,0:T(8,128)} %all-reduce.19.cloned.1.call-done) | copy-start | bytes 393220
  466.2 8.0 %copy-start.14 = (f32[256,128]{1,0:T(8,128)S(1)}, f32[256,128]{1,0:T(8,128)}, u32[]{:S(2)}) copy-start(f32[256,128]{1,0:T(8,128)} %all-reduce.21.cloned.1.call-done) | copy-start | bytes 393220
  466.2 9.6 %copy-start.15 = (f32[3,2,1024]{2,1,0:T(2,128)S(1)}, f32[3,2,1024]{2,1,0:T(2,128)}, u32[]{:S(2)}) copy-start(f32[3,2,1024]{2,1,0:T(2,128)} %param.7) | copy-start | bytes 73732
  468.1 69.1 %collective-permute-start = (f32[128,3,1,1024]{3,0,2,1:T(8,128)}, f32[128,3,1,1024]{3,0,2,1:T(8,128)}, u32[]{:S(2)}, u32[]{:S(2)}) collective-permute-start(f32[128,3,1,1024]{3,0,2,1:T(8,128)} %get-tuple-element.21), channel_id=1, source_target_pairs={{0,4},{4,8},{8,12},{12,16},{16,20},{20,24},{24,28},{1,5},{5,9},{9,... | collective-permute-start | bytes 4718600 | tf_op jit(solution)/shard_map/ppermute | solution.py:17
  472.6 64.6 %collective-permute-start.1 = (f32[128,3,1,1024]{3,0,2,1:T(8,128)}, f32[128,3,1,1024]{3,0,2,1:T(8,128)}, u32[]{:S(2)}, u32[]{:S(2)}) collective-permute-start(f32[128,3,1,1024]{3,0,2,1:T(8,128)} %get-tuple-element.22), channel_id=1, source_target_pairs={{4,0},{8,4},{12,8},{16,12},{20,16},{24,20},{28,24},{5,1},{9,5},{13... | collective-permute-start | bytes 4718600 | tf_op jit(solution)/shard_map/ppermute | solution.py:18
  475.0 0.9 copy-start.1
  475.8 13.0 %slice-start = ((s8[6291456]{0:T(1024)(128)(4,1)}), s8[4194304]{0:T(1024)(128)(4,1)S(1)}, s32[]{:S(2)}) async-start(s8[6291456]{0:T(1024)(128)(4,1)} %bitcast.108), calls=%async_computation.11 | async-start | bytes 8388608
  479.0 9.9 %slice-start.1 = ((s8[6291456]{0:T(1024)(128)(4,1)}), s8[2097152]{0:T(1024)(128)(4,1)S(1)}, s32[]{:S(2)}) async-start(s8[6291456]{0:T(1024)(128)(4,1)} %bitcast.108), calls=%async_computation.12 | async-start | bytes 4194304
  549.8 3.2 copy-start.6
  549.8 1.6 copy-start.8
  549.8 1.9 copy-start.11
  551.2 1.8 copy-start.4
  553.0 7.3 %copy-start.9 = (f32[128,1,2,1024]{3,0,2,1:T(8,128)}, f32[128,1,2,1024]{3,0,2,1:T(8,128)S(1)}, u32[]{:S(2)}) copy-start(f32[128,1,2,1024]{3,0,2,1:T(8,128)S(1)} %add_bitcast_fusion) | copy-start | bytes 3145732
  561.1 4.5 copy-start.2
  561.1 6.0 copy-start.5
  561.1 6.0 copy-start.7
  561.1 6.0 copy-start.10
Sparse Core Ops, SparseCore 0:
  10.1 31.2 all-gather.3
  52.3 69.6 all-reduce.18
  133.4 37.2 reduce-scatter.2
  173.1 28.5 all-gather.5
  212.5 69.6 all-reduce.20
  293.6 37.2 reduce-scatter.4
  333.1 28.5 all-gather.7
  368.1 68.4 all-reduce.22
  561.2 72.4 all-reduce.24
where the time goes:
time: 652 us; the launch traced here: 643 us
  waiting for transfers between devices  421 us (65%)
  matrix products  90.2 us (14%)
  other arithmetic  38.7 us (6%)
  blocking collectives  37.2 us (6%)
  local copies, waits for them, and re-layouts  34 us (5%)
  between operations  14.7 us (2%)
  starting transfers between devices  6.98 us (1%)
    psum x2, waiting for transfers between devices, shards(): coef_part = lax.psum(partial_value, 'grid')  124 us
    reduce_scatter x2, waiting for transfers between devices, shards(): lax.psum_scatter(combine_rows(coef_part, basis), 'cols', scatter_dimensio...  74.4 us
    psum x1, waiting for transfers between devices, shards(): gram_sum = lax.psum(cells_dot(finished, finished) / unknowns, 'grid')  66.2 us
    dot_general x9, matrix products, cells_dot(): lax.dot_general(left_flat, right_flat, (((1,), (1,)), ((), ())), precisio...  62.8 us
    all_gather x2, waiting for transfers between devices, shards(): lax.all_gather(current, 'cols', axis=0, tiled=True)  60.5 us
    ppermute x1, waiting for transfers between devices, padded(): before = lax.ppermute(last, axis, up)  41 us
    psum x1, blocking collectives, shards(): cross_terms, block_terms = lax.psum((cross_part, block_part), 'grid')  37.2 us
    all_gather x1, waiting for transfers between devices, shards(): finished = lax.all_gather(current, 'cols', axis=0, tiled=True)  28.2 us
  transfers between devices with their start and end apart: 11, of which 10 were waited for; matrix products, arithmetic and copies ran while one was open for 7% of the time, Pallas kernels for 0%

commit v1 on v0

--- a/solution.py
+++ b/solution.py
@@ -144,7 +144,7 @@
     coefficients = jnp.zeros((basis_cols, total_snap), jnp.float32)
     for sweep_index in range(2):
         partial_value = cells_dot(basis, lax.all_gather(current, "cols", axis=0, tiled=True))
-        coef_part = lax.psum(partial_value, "grid")
+        coef_part = jnp.sum(lax.all_gather(partial_value, "grid"), axis=0)
         current = current - lax.psum_scatter(
             combine_rows(coef_part, basis), "cols", scatter_dimension=0, tiled=True
         )

time: 652 us -> 594 us (0.911)
  waiting for transfers between devices: 421 us -> 359 us
    psum x2 -> x0, waiting for transfers between devices: 124 us -> none  [shards(): coef_part = lax.psum(partial_value, 'grid')]
    all_gather x0 -> x2, waiting for transfers between devices: none -> 64.2 us  [shards(): coef_part = jnp.sum(lax.all_gather(partial_value, 'grid'), axis=0)]
  transfers between devices with their start and end apart: 11 -> 11, of which waited for: 10 -> 10; matrix products, arithmetic and copies ran while one was open for 7% -> 8% of each run, Pallas kernels for 0% -> 0%
where the time goes in v1:
time: 594 us; the launch traced here: 585 us
  waiting for transfers between devices  359 us (60%)
  matrix products  91.3 us (15%)
  other arithmetic  40.3 us (7%)
  blocking collectives  37.2 us (6%)
  local copies, waits for them, and re-layouts  35.7 us (6%)
  between operations  14.5 us (2%)
  starting transfers between devices  7.45 us (1%)
    reduce_scatter x2, waiting for transfers between devices, shards(): lax.psum_scatter(combine_rows(coef_part, basis), 'cols', scatter_dimensio...  73.3 us
    psum x1, waiting for transfers between devices, shards(): gram_sum = lax.psum(cells_dot(finished, finished) / unknowns, 'grid')  66 us
    dot_general x9, matrix products, cells_dot(): lax.dot_general(left_flat, right_flat, (((1,), (1,)), ((), ())), precisio...  64.3 us
    all_gather x2, waiting for transfers between devices, shards(): coef_part = jnp.sum(lax.all_gather(partial_value, 'grid'), axis=0)  64.2 us
    all_gather x2, waiting for transfers between devices, shards(): lax.all_gather(current, 'cols', axis=0, tiled=True)  60.5 us
    ppermute x1, waiting for transfers between devices, padded(): before = lax.ppermute(last, axis, up)  39.9 us
    psum x1, blocking collectives, shards(): cross_terms, block_terms = lax.psum((cross_part, block_part), 'grid')  37.2 us
    all_gather x1, waiting for transfers between devices, shards(): finished = lax.all_gather(current, 'cols', axis=0, tiled=True)  28.6 us
  transfers between devices with their start and end apart: 11, of which 10 were waited for; matrix products, arithmetic and copies ran while one was open for 8% of the time, Pallas kernels for 0%

profile of v1, /device:TPU:0, one launch (start us, length us, event | category | flops | bytes accessed | tf_op | source)
XLA Modules:
  0.0 585.3 jit_solution(11706559846571948665)
XLA Ops:
  7.2 2.3 copy.71
  9.5 31.9 %all-gather.8.cloned.1.call-done = f32[128,3,2,1024]{3,0,2,1:T(8,128)} async-done(((f32[32,3,2,1024]{3,0,2,1:T(8,128)}), f32[128,3,2,1024]{3,0,2,1:T(8,128)}) %all-gather.8.cloned.1.call-update) | async-done | bytes 3145744 | tf_op jit(solution)/shard_map/all_gather | solution.py:146
  41.4 10.8 %fusion.23 = f32[256,128]{1,0:T(8,128)} fusion(f32[128,3,2,1024]{3,0,2,1:T(8,128)} %all-gather.8.cloned.1.call-done, f32[256,3,2,1024]{3,2,1,0:T(2,128)} %param.5), kind=kOutput, calls=%fused_computation.28 | convolution fusion | flops 2415919104 | bytes 9568256 | tf_op jit(solution)/shard_map/dot_general | solution.py:26
  52.2 9.0 %reshape.49 = f32[256,6144]{1,0:T(8,128)} reshape(f32[256,3,2,1024]{3,2,1,0:T(2,128)} %param.5) | data formatting | bytes 12582912 | tf_op jit(solution)/shard_map/reshape | solution.py:24
  61.2 6.6 %copy.69 = f32[6144,256]{1,0:T(8,128)} copy(f32[6144,256]{0,1:T(8,128)} %bitcast.122) | data formatting | bytes 12582912 | tf_op jit(solution)/shard_map/dot_general | solution.py:37
  67.8 24.8 %all-gather.14.cloned.1.call-done = f32[2048,128]{1,0:T(8,128)} async-done(((f32[256,128]{1,0:T(8,128)}), f32[2048,128]{1,0:T(8,128)}) %all-gather.14.cloned.1.call-update) | async-done | bytes 1048592 | tf_op jit(solution)/shard_map/all_gather | solution.py:147
  92.6 1.3 reduce_sum.27
  93.9 11.2 %fusion.63 = f32[128,3,2,1024]{3,0,2,1:T(8,128)} fusion(f32[3,2,1024,256]{3,2,1,0:T(8,128)} %bitcast.120, f32[256,128]{1,0:T(8,128)S(1)} %reduce_sum.27), kind=kOutput, calls=%fused_computation.62 | convolution fusion | flops 2415919104 | bytes 9568256 | tf_op jit(solution)/shard_map/dot_general | solution.py:37
  105.0 0.5 all-gather.10.cloned.1.call-start
  105.6 36.4 %reduce-scatter.3.cloned.1.call-done = f32[32,3,2,1024]{3,0,2,1:T(8,128)} async-done(((f32[128,3,2,1024]{3,0,2,1:T(8,128)}), f32[32,3,2,1024]{3,0,2,1:T(8,128)}) %reduce-scatter.3.cloned.1.call-update) | async-done | bytes 786448 | tf_op jit(solution)/shard_map/reduce_scatter | solution.py:148
  141.9 2.3 copy_subtract_fusion
  144.3 28.6 %all-gather.10.cloned.1.call-done = f32[128,3,2,1024]{3,0,2,1:T(8,128)} async-done(((f32[32,3,2,1024]{3,0,2,1:T(8,128)}), f32[128,3,2,1024]{3,0,2,1:T(8,128)}) %all-gather.10.cloned.1.call-update) | async-done | bytes 3145744 | tf_op jit(solution)/shard_map/all_gather | solution.py:146
  172.9 11.4 %fusion.26 = f32[256,128]{0,1:T(8,128)} fusion(f32[128,3,2,1024]{3,0,2,1:T(8,128)} %all-gather.10.cloned.1.call-done, f32[256,3,2,1024]{3,2,1,0:T(2,128)} %param.5), kind=kOutput, calls=%fused_computation.29 | convolution fusion | flops 2415919104 | bytes 9568256 | tf_op jit(solution)/shard_map/dot_general | solution.py:26
  184.3 0.2 reduce-scatter.5.cloned.1.call-start
  184.6 39.5 %all-gather.16.cloned.1.call-done = f32[2048,128]{0,1:T(8,128)} async-done(((f32[256,128]{0,1:T(8,128)}), f32[2048,128]{0,1:T(8,128)}) %all-gather.16.cloned.1.call-update) | async-done | bytes 1048592 | tf_op jit(solution)/shard_map/all_gather | solution.py:147
  224.0 1.6 copy.96
  225.6 0.3 bitcast_reduce_fusion
  225.9 10.9 %fusion.61 = f32[128,3,2,1024]{3,0,2,1:T(8,128)} fusion(f32[3,2,1024,256]{3,2,1,0:T(8,128)} %bitcast.121, f32[256,128]{0,1:T(8,128)S(1)} %bitcast_reduce_fusion), kind=kOutput, calls=%fused_computation.60 | convolution fusion | flops 2415919104 | bytes 9568256 | tf_op jit(solution)/shard_map/dot_general | solution.py:37
  236.8 0.0 all-gather.12.cloned.1.call-start
  236.9 36.9 %reduce-scatter.5.cloned.1.call-done = f32[32,3,2,1024]{3,0,2,1:T(8,128)} async-done(((f32[128,3,2,1024]{3,0,2,1:T(8,128)}), f32[32,3,2,1024]{3,0,2,1:T(8,128)}) %reduce-scatter.5.cloned.1.call-update) | async-done | bytes 786448 | tf_op jit(solution)/shard_map/reduce_scatter | solution.py:148
  273.8 2.1 sub.76
  276.0 28.6 %all-gather.12.cloned.1.call-done = f32[128,3,2,1024]{3,0,2,1:T(8,128)} async-done(((f32[32,3,2,1024]{3,0,2,1:T(8,128)}), f32[128,3,2,1024]{3,0,2,1:T(8,128)}) %all-gather.12.cloned.1.call-update) | async-done | bytes 3145744 | tf_op jit(solution)/shard_map/all_gather | solution.py:152
  304.6 6.3 %fusion.42 = f32[128,128]{0,1:T(8,128)} fusion(f32[128,3,2,1024]{3,0,2,1:T(8,128)} %all-gather.12.cloned.1.call-done), kind=kOutput, calls=%fused_computation.35 | convolution fusion | flops 1207975936 | bytes 3211264 | tf_op jit(solution)/shard_map/dot_general | solution.py:26
  310.9 0.3 all-reduce.19.cloned.1.call-start
  311.2 2.3 copy.75
  313.5 66.0 %all-reduce.17.cloned.1.call-done = f32[128,128]{0,1:T(8,128)} async-done(((f32[128,128]{0,1:T(8,128)}), f32[128,128]{0,1:T(8,128)}) %all-reduce.17.cloned.1.call-update) | async-done | bytes 65552 | tf_op jit(solution)/shard_map/psum | solution.py:155
  379.6 0.9 copy.74
  380.5 0.9 fusion.67
  381.4 11.7 %cholesky.17 = f32[128,128]{1,0:T(8,128)S(1)} custom-call(f32[128,128]{1,0:T(8,128)S(1)} %fusion.67), custom_call_target="Cholesky" | custom-call | tf_op jit(solution)/shard_map/jit(cholesky)/cholesky | solution.py:156
  393.1 0.6 compare_reduce_fusion
  393.8 0.7 fusion.65
  394.4 9.8 %custom-call.7 = f32[1,128,128]{1,2,0:T(8,128)S(1)} custom-call(f32[1,128,128]{2,1,0:T(8,128)S(1)} %fusion.65), custom_call_target="InvertDiagBlocksLowerTriangular" | custom-call | tf_op jit(solution)/shard_map/jit(_solve_triangular)/triangular_solve | solution.py:157
  404.2 0.2 convolution_bitcast_fusion
  404.5 4.7 fusion.10
  409.2 1.8 fusion.75
  411.0 4.5 collective-permute-start
  415.6 1.7 collective-permute-start.1
  417.3 0.1 select_reduce_fusion
  417.4 0.1 copy.76
  417.5 0.7 add.128
  418.2 0.1 constant_dynamic-slice_fusion
  418.2 0.9 copy-done.1
  419.1 4.0 fusion.44
  423.2 9.9 %fusion.37 = f32[1,256,128]{1,2,0:T(8,128)S(1)} fusion(f32[256,3,2,1024]{3,2,1,0:T(2,128)} %param.5, f32[128,3,2,1024]{3,0,2,1:T(8,128)S(1)} %fusion.10, f32[2,1024]{1,0:T(2,128)S(1)} %select_reduce_fusion), kind=kOutput, calls=%fused_computation.32 | convolution fusion | flops 2416705536 | bytes 9576448 | tf_op jit(solution)/shard_map/dot_general | solution.py:26
  433.1 7.2 %fusion.32 = f32[1,256,128]{1,2,0:T(8,128)S(1)} fusion(f32[256,3,2,1024]{3,2,1,0:T(2,128)S(1)} %bitcast.119, f32[128,3,2,1024]{3,0,2,1:T(8,128)S(1)} %fusion.10, f32[3,2,1024]{2,1,0:T(2,128)S(1)} %copy-done.13), kind=kOutput, calls=%fused_computation.31 | convolution fusion | flops 2416705536 | bytes 9592832 | tf_op jit(solution)/shard_map/dot_general | solution.py:26
  440.3 39.9 %collective-permute-done = f32[128,3,1,1024]{3,0,2,1:T(8,128)} collective-permute-done((f32[128,3,1,1024]{3,0,2,1:T(8,128)}, f32[128,3,1,1024]{3,0,2,1:T(8,128)}, u32[]{:S(2)}, u32[]{:S(2)}) %collective-permute-start) | collective-permute-done | bytes 1572896 | tf_op jit(solution)/shard_map/ppermute | solution.py:17
  480.1 2.7 pad_maximum_fusion
  482.9 1.1 slice_bitcast_fusion
  484.0 2.6 fusion.76
  486.6 2.5 fusion.77
  489.1 0.4 pad_subtract_fusion
  489.4 3.4 fusion.59
  492.8 1.4 fusion.54
  494.2 0.2 copy-done.8
  494.4 0.3 copy-done.11
  494.7 1.2 add_bitcast_fusion
  496.0 7.2 %fusion.29 = f32[1,256,128]{1,2,0:T(8,128)S(1)} fusion(f32[256,3,2,1024]{3,2,1,0:T(2,128)S(1)} %bitcast.119, f32[128,1,2,1024]{3,0,2,1:T(8,128)S(1)} %add_bitcast_fusion, f32[128,1,2,1024]{3,0,2,1:T(8,128)S(1)} %fusion.54, f32[128,1,2,1024]{3,0,2,1:T(8,128)S(1)} %get-tuple-element.27), kind=kOutput, calls=%fused_computation.30 | convolution fusion | flops 2417491968 | bytes 9568256 | tf_op jit(solution)/shard_map/dot_general | solution.py:26
  503.2 0.8 pad_maximum_fusion.8
  504.1 4.4 fusion.47
  508.5 1.5 copy.80
  510.0 3.1 fusion.43
  513.2 37.2 %psum.23 = f32[3,32,128]{2,1,0:T(8,128)} all-reduce(f32[3,32,128]{2,1,0:T(8,128)S(1)} %maximum_multiply_fusion), channel_id=1, replica_groups=mesh['grid'=8,'cols'=4] {'grid'}, use_global_device_ids=true, to_apply=%region_9.10 | all-reduce | flops 12288 | bytes 98304 | tf_op jit(solution)/shard_map/psum | solution.py:176
  550.4 26.2 %all-reduce.19.cloned.1.call-done = f32[3,256,128]{1,2,0:T(8,128)} async-done(((f32[3,256,128]{1,2,0:T(8,128)}), f32[3,256,128]{1,2,0:T(8,128)}) %all-reduce.19.cloned.1.call-update) | async-done | bytes 393232 | tf_op jit(solution)/shard_map/psum | solution.py:176
  576.6 1.9 copy.81
  (52 shorter events, 0.5 us)
Async XLA Ops:
  7.2 34.2 %all-gather.8.cloned.1.call-start = ((), (), s32[]{:S(2)}) async-start(), calls=%async_computation.2 | async-start | bytes 3932160 | tf_op jit(solution)/shard_map/all_gather | solution.py:146
  9.5 83.1 %all-gather.14.cloned.1.call-start = ((), (), s32[]{:S(2)}) async-start(), calls=%async_computation.9 | async-start | bytes 1179648 | tf_op jit(solution)/shard_map/all_gather | solution.py:147
  52.2 89.7 %reduce-scatter.3.cloned.1.call-start = ((), (), s32[]{:S(2)}) async-start(), calls=%async_computation.3 | async-start | bytes 3932160 | tf_op jit(solution)/shard_map/reduce_scatter | solution.py:148
  105.0 36.9 %copy-start.12 = (f32[32,3,2,1024]{3,2,1,0:T(2,128)S(1)}, f32[32,3,2,1024]{3,2,1,0:T(2,128)}, u32[]{:S(2)}) copy-start(f32[32,3,2,1024]{3,2,1,0:T(2,128)} %param.6) | copy-start | bytes 2359300
  105.0 67.9 %all-gather.10.cloned.1.call-start = ((), (), s32[]{:S(2)}) async-start(), calls=%async_computation.4 | async-start | bytes 3932160 | tf_op jit(solution)/shard_map/all_gather | solution.py:146
  144.3 79.8 %all-gather.16.cloned.1.call-start = ((), (), s32[]{:S(2)}) async-start(), calls=%async_computation.10 | async-start | bytes 1179648 | tf_op jit(solution)/shard_map/all_gather | solution.py:147
  184.3 89.5 %reduce-scatter.5.cloned.1.call-start = ((), (), s32[]{:S(2)}) async-start(), calls=%async_computation.5 | async-start | bytes 3932160 | tf_op jit(solution)/shard_map/reduce_scatter | solution.py:148
  236.8 37.0 %copy-start.3 = (f32[32,3,2,1024]{3,0,2,1:T(8,128)S(1)}, f32[32,3,2,1024]{3,0,2,1:T(8,128)}, u32[]{:S(2)}) copy-start(f32[32,3,2,1024]{3,0,2,1:T(8,128)} %copy_subtract_fusion) | copy-start | bytes 2359300
  236.8 67.8 %all-gather.12.cloned.1.call-start = ((), (), s32[]{:S(2)}) async-start(), calls=%async_computation.6 | async-start | bytes 3932160 | tf_op jit(solution)/shard_map/all_gather | solution.py:152
  275.9 103.6 %all-reduce.17.cloned.1.call-start = ((), (), s32[]{:S(2)}) async-start(), calls=%async_computation.7 | async-start | bytes 131072 | tf_op jit(solution)/shard_map/psum | solution.py:155
  304.6 6.6 %copy-start = (f32[128,3,2,1024]{3,0,2,1:T(8,128)S(1)}, f32[128,3,2,1024]{3,0,2,1:T(8,128)}, u32[]{:S(2)}) copy-start(f32[128,3,2,1024]{3,0,2,1:T(8,128)} %all-gather.12.cloned.1.call-done) | copy-start | bytes 9437188
  310.9 265.7 %all-reduce.19.cloned.1.call-start = ((), (), s32[]{:S(2)}) async-start(), calls=%async_computation.8 | async-start | bytes 786432 | tf_op jit(solution)/shard_map/psum | solution.py:176
  409.1 8.1 %copy-start.14 = (s32[2,1024]{1,0:T(2,128)S(1)}, s32[2,1024]{1,0:T(2,128)}, u32[]{:S(2)}) copy-start(s32[2,1024]{1,0:T(2,128)} %param.8) | copy-start | bytes 24580
  409.2 8.1 %copy-start.15 = (f32[8]{0:T(128)S(1)}, f32[8]{0:T(128)}, u32[]{:S(2)}) copy-start(f32[8]{0:T(128)} %param.9) | copy-start | bytes 100
  411.0 69.1 %collective-permute-start = (f32[128,3,1,1024]{3,0,2,1:T(8,128)}, f32[128,3,1,1024]{3,0,2,1:T(8,128)}, u32[]{:S(2)}, u32[]{:S(2)}) collective-permute-start(f32[128,3,1,1024]{3,0,2,1:T(8,128)} %get-tuple-element.29), channel_id=1, source_target_pairs={{0,4},{4,8},{8,12},{12,16},{16,20},{20,24},{24,28},{1,5},{5,9},{9,... | collective-permute-start | bytes 4718600 | tf_op jit(solution)/shard_map/ppermute | solution.py:17
  415.6 64.6 %collective-permute-start.1 = (f32[128,3,1,1024]{3,0,2,1:T(8,128)}, f32[128,3,1,1024]{3,0,2,1:T(8,128)}, u32[]{:S(2)}, u32[]{:S(2)}) collective-permute-start(f32[128,3,1,1024]{3,0,2,1:T(8,128)} %get-tuple-element.30), channel_id=1, source_target_pairs={{4,0},{8,4},{12,8},{16,12},{20,16},{24,20},{28,24},{5,1},{9,5},{13... | collective-permute-start | bytes 4718600 | tf_op jit(solution)/shard_map/ppermute | solution.py:18
  418.2 0.9 copy-start.1
  419.1 13.9 %slice-start = ((s8[6291456]{0:T(1024)(128)(4,1)}), s8[4194304]{0:T(1024)(128)(4,1)S(1)}, s32[]{:S(2)}) async-start(s8[6291456]{0:T(1024)(128)(4,1)} %bitcast.118), calls=%async_computation.11 | async-start | bytes 8388608
  423.1 9.9 %slice-start.1 = ((s8[6291456]{0:T(1024)(128)(4,1)}), s8[2097152]{0:T(1024)(128)(4,1)S(1)}, s32[]{:S(2)}) async-start(s8[6291456]{0:T(1024)(128)(4,1)} %bitcast.118), calls=%async_computation.12 | async-start | bytes 4194304
  423.2 9.9 %copy-start.13 = (f32[3,2,1024]{2,1,0:T(2,128)S(1)}, f32[3,2,1024]{2,1,0:T(2,128)}, u32[]{:S(2)}) copy-start(f32[3,2,1024]{2,1,0:T(2,128)} %param.7) | copy-start | bytes 73732
  492.8 3.2 copy-start.6
  492.8 1.6 copy-start.8
  492.8 1.9 copy-start.11
  494.2 1.8 copy-start.4
  496.0 7.3 %copy-start.9 = (f32[128,1,2,1024]{3,0,2,1:T(8,128)}, f32[128,1,2,1024]{3,0,2,1:T(8,128)S(1)}, u32[]{:S(2)}) copy-start(f32[128,1,2,1024]{3,0,2,1:T(8,128)S(1)} %add_bitcast_fusion) | copy-start | bytes 3145732
  504.1 4.5 copy-start.2
  504.1 6.0 %copy-start.5 = (f32[128,1,2,1024]{3,0,2,1:T(8,128)S(1)}, f32[128,1,2,1024]{3,0,2,1:T(8,128)}, u32[]{:S(2)}) copy-start(f32[128,1,2,1024]{3,0,2,1:T(8,128)} %copy-done.4) | copy-start | bytes 3145732
  504.1 6.0 %copy-start.7 = (f32[128,1,2,1024]{3,0,2,1:T(8,128)S(1)}, f32[128,1,2,1024]{3,0,2,1:T(8,128)}, u32[]{:S(2)}) copy-start(f32[128,1,2,1024]{3,0,2,1:T(8,128)} %copy-done.6) | copy-start | bytes 3145732
  504.1 6.0 %copy-start.10 = (f32[128,1,2,1024]{3,0,2,1:T(8,128)S(1)}, f32[128,1,2,1024]{3,0,2,1:T(8,128)}, u32[]{:S(2)}) copy-start(f32[128,1,2,1024]{3,0,2,1:T(8,128)} %copy-done.9) | copy-start | bytes 3145732
Sparse Core Ops, SparseCore 0:
  10.1 31.2 all-gather.7
  52.3 40.2 all-gather.13
  105.2 36.7 reduce-scatter.2
  144.4 28.5 all-gather.9
  184.5 39.5 all-gather.15
  236.9 36.8 reduce-scatter.4
  276.0 28.5 all-gather.11
  311.0 68.4 all-reduce.16
  504.2 72.4 all-reduce.18
